TPU v7x, 128 devices: a whole 4x4x4 slice. The times are simulated.
128 devices in a mesh: row: 8 (over z, core), col: 16 (over y, x).
Axes of the slice: x: 4, y: 4, z: 4, core: 2. Of those that a mesh axis runs over, the one named last changes fastest.
Arguments:
- working: float32 [8, 8, 256, 4, 16, 256], P(None, 'row', None, None, 'col'), may hold values from -6 to 6
- factor_panel: float32 [2, 8, 8, 256, 256], P(None, None, 'row'), may hold values from -0.12 to 2, as said below
Outputs:
- gram_part: float32 [8, 8, 256, 4, 16, 256], P(None, 'row', None, None, 'col')
- finished_columns: float32 [4, 8, 256, 16, 8, 128], P(None, None, None, 'col', 'row')
Inputs may be any that keep to these rules, and one draw needn't show every extreme that they name: factor_panel holds a lower-triangular factor: entries above the factor's diagonal are zero and its diagonal entries lie between 1 and 2.
All inputs are finite; a program needn't handle non-finite values.
Results may differ from a plain program's by a relative error of at most 0.0001.
Values sent between devices are 32-bit elements; how exact they have to be, the bound alone decides.
A program may use at most 192 MiB of HBM per device.

v0:
```python
import jax
import jax.numpy as jnp
from jax import lax
from jax.sharding import PartitionSpec as P

BLK = 256
K = 30
STEPS = 2


def picked(value, axis, root):
    return lax.dynamic_index_in_dim(lax.all_gather(value, axis), root, 0, keepdims=False)


def per_device(working, factor_panel):
    row_count = lax.axis_size("row")
    col_count = lax.axis_size("col")
    row_index = lax.axis_index("row")
    blocks_rows = working.shape[0]
    width = working.shape[2]
    blocks_cols = working.shape[3]
    matrix_rows = working.reshape(blocks_rows, width, blocks_cols * width)
    global_block = jnp.arange(blocks_rows) * row_count + row_index

    def solve_row(slab, step_index):
        target = K + step_index
        owner = target % row_count
        diagonal = jnp.tril(factor_panel[step_index, target // row_count, 0])
        diagonal = jnp.where(row_index == owner, diagonal, jnp.eye(width, dtype=jnp.float32))
        solved = lax.linalg.triangular_solve(diagonal, slab, left_side=True, lower=True)
        return picked(solved, "row", owner)

    def eliminate(rows_part, blocks_part, column_part, solved, step_index):
        target = K + step_index
        updated = rows_part - jnp.einsum(
            "rab,bc->rac", column_part, solved, precision=lax.Precision.HIGHEST
        )
        below = (blocks_part > target)[:, None, None]
        here = (blocks_part == target)[:, None, None]
        return jnp.where(below, updated, jnp.where(here, solved[None], rows_part))

    solved_list = []
    solved = solve_row(matrix_rows[K // row_count], 0)
    for step_index in range(STEPS):
        solved_list.append(solved)
        if step_index + 1 < STEPS:
            slot = (K + step_index + 1) // row_count
            next_slab = eliminate(
                matrix_rows[slot : slot + 1],
                global_block[slot : slot + 1],
                factor_panel[step_index, slot : slot + 1, 0],
                solved,
                step_index,
            )
            following = solve_row(next_slab[0], step_index + 1)
        matrix_rows = eliminate(
            matrix_rows, global_block, factor_panel[step_index, :, 0], solved, step_index
        )
        if step_index + 1 < STEPS:
            solved = following
    stacked = jnp.concatenate(solved_list, 0)
    depth = stacked.shape[0]
    owners_count = col_count // row_count
    gathered = lax.all_gather(
        stacked.reshape(depth, blocks_cols, 1, width), "col", axis=2, tiled=True
    )
    gathered = gathered.reshape(depth, blocks_cols, owners_count, row_count, width)
    chosen = lax.dynamic_index_in_dim(gathered, row_index, 3, keepdims=False)
    row_panels = chosen.reshape(depth, blocks_rows * width)
    gram = lax.dot_general(
        row_panels, stacked, (((0,), (0,)), ((), ())), precision=lax.Precision.HIGHEST
    )
    gram = (gram * (1.0 / (STEPS * BLK))).reshape(blocks_rows, 1, width, blocks_cols, 1, width)
    finished_count = (K + STEPS) // row_count
    finished = matrix_rows[:finished_count].reshape(finished_count, 1, width, 1, row_count, -1)
    moved = lax.all_to_all(finished, "row", split_axis=4, concat_axis=1, tiled=True)
    return (gram, moved)


def solution(mesh):
    placed = (P(None, "row", None, None, "col", None), P(None, None, "row", None, None))
    return jax.shard_map(
        per_device,
        mesh=mesh,
        in_specs=placed,
        out_specs=(
            P(None, "row", None, None, "col", None),
            P(None, None, None, "col", "row", None),
        ),
        check_vma=False,
    )
```

profile of v0, /device:TPU:1, one launch (start us, length us, event | category | flops | bytes accessed | tf_op | source)
XLA Modules:
  0.0 434.1 jit_solution(2634957382837194387)
XLA Ops:
  7.2 0.0 all-gather.8.cloned.1.call-start
  7.2 1.1 fusion.16
  8.3 0.1 broadcast.89
  8.4 3.8 while.4
  8.4 0.6 fusion.36
  9.0 1.3 bitcast_dynamic-update-slice_fusion.4
  10.3 0.6 fusion.36
  10.9 1.3 bitcast_dynamic-update-slice_fusion.4
  12.2 19.7 %custom-call.4 = f32[2,128,128]{1,2,0:T(8,128)S(1)} custom-call(f32[2,128,128]{2,1,0:T(8,128)S(1)} %get-tuple-element.17), custom_call_target="InvertDiagBlocksLowerTriangular" | custom-call | tf_op jit(solution)/shard_map/triangular_solve/custom-call.1 | solution.py:30
  31.9 4.2 slice_reduce_fusion
  36.0 0.2 copy.57
  36.3 0.6 fusion.13
  36.9 0.6 convolution_subtract_fusion.1
  37.5 0.6 fusion.22
  38.1 1.0 pad_maximum_fusion.1
  39.2 0.0 all-gather.8.cloned.1.call-update
  39.2 0.6 all-gather.10.cloned.1.call-start
  39.8 0.6 slice.46
  41.7 0.5 slice.47
  42.2 4.1 while.5
  42.2 0.7 fusion.37
  42.9 1.3 bitcast_dynamic-update-slice_fusion.5
  44.3 0.7 fusion.37
  44.9 1.3 bitcast_dynamic-update-slice_fusion.5
  46.3 19.7 %custom-call.5 = f32[2,128,128]{1,2,0:T(8,128)S(1)} custom-call(f32[2,128,128]{2,1,0:T(8,128)S(1)} %get-tuple-element.18), custom_call_target="InvertDiagBlocksLowerTriangular" | custom-call | tf_op jit(solution)/shard_map/triangular_solve/custom-call.1 | solution.py:30
  66.0 27.0 %all-gather.8.cloned.1.call-done = f32[2048,1024]{1,0:T(8,128)} async-done(((f32[256,1024]{1,0:T(8,128)}), f32[2048,1024]{1,0:T(8,128)}) %all-gather.8.cloned.1.call-update) | async-done | bytes 8388624 | tf_op jit(solution)/shard_map/all_gather | solution.py:12
  93.0 2.9 fusion.8
  95.8 0.6 fusion.11
  96.5 0.6 convolution_subtract_fusion
  97.1 0.6 fusion.20
  97.7 1.0 pad_maximum_fusion.2
  98.7 0.0 all-gather.10.cloned.1.call-update
  98.8 0.2 all-gather.6.cloned.1.call-start
  99.0 1.3 slice.86
  100.3 0.5 concatenate.13
  100.8 1.2 copy.38
  101.9 47.1 %all-gather.10.cloned.1.call-done = f32[2048,1024]{1,0:T(8,128)} async-done(((f32[256,1024]{1,0:T(8,128)}), f32[2048,1024]{1,0:T(8,128)}) %all-gather.10.cloned.1.call-update) | async-done | bytes 8388624 | tf_op jit(solution)/shard_map/all_gather | solution.py:12
  149.1 1.3 slice.92
  150.4 0.5 concatenate.14
  150.9 0.2 copy.39
  151.1 2.8 pad_maximum_fusion
  153.9 0.0 all-gather.6.cloned.1.call-update
  153.9 20.9 %copy.42 = f32[8,1,256,4,1,256]{2,5,3,0,4,1:T(8,128)} copy(f32[8,1,256,4,1,256]{5,4,3,2,1,0:T(1,128)} %param.4) | data formatting | bytes 16777216 | tf_op args[0]
  174.8 0.3 copy.45
  175.1 17.2 %convolution_bitcast_fusion.1 = f32[8,256,1024]{1,2,0:T(8,128)} fusion(f32[2,8,1,256,256]{4,3,1,2,0:T(8,128)} %bitcast.110, f32[2048,1024]{1,0:T(8,128)} %all-gather.8.cloned.1.call-done), kind=kOutput, calls=%fused_computation.11 | convolution fusion | flops 6442450944 | bytes 11534336 | tf_op jit(solution)/shard_map/rab,bc->rac/dot_general | solution.py:35
  192.3 1.3 copy.48
  193.6 0.0 copy-start
  193.6 0.0 copy-start.1
  193.6 16.5 %convolution_bitcast_fusion = f32[8,256,1024]{1,2,0:T(8,128)S(1)} fusion(f32[2,8,1,256,256]{4,3,1,2,0:T(8,128)} %bitcast.111, f32[2048,1024]{1,0:T(8,128)} %all-gather.10.cloned.1.call-done), kind=kOutput, calls=%fused_computation.10 | convolution fusion | flops 6442450944 | bytes 11534336 | tf_op jit(solution)/shard_map/rab,bc->rac/dot_general | solution.py:35
  210.2 0.0 copy-done
  210.2 0.0 copy-done.1
  210.2 4.9 %fusion = f32[4,256,1024]{1,2,0:T(8,128)} fusion(f32[8,256,1024]{1,2,0:T(8,128)S(1)} %convolution_bitcast_fusion, f32[8,256,1024]{1,2,0:T(8,128)S(1)} %copy-done, f32[8,256,1024]{1,2,0:T(8,128)} %bitcast.108, f32[256,1024]{0,1:T(8,128)S(1)} %copy-done.1, f32[256,1024]{0,1:T(8,128)S(1)} %copy.45, pred[4]{0:T(512)(128)(4,1)S(1)} %bitcast.117, ...), kind=kLoop, calls=%fused_computation.7 | loop fusion | flops 6291456 | bytes 18874384 | tf_op jit(solution)/shard_map/jit(_where)/select_n | solution.py:40
  215.1 5.7 %copy.49 = f32[4,1,256,1,8,128]{5,2,0,3,1,4:T(8,128)} copy(f32[4,1,256,1,8,128]{2,5,4,0,3,1:T(8,128)} %bitcast.109) | data formatting | bytes 8388608 | tf_op jit(solution)/shard_map/reshape | solution.py:75
  220.9 4.7 %all-to-all-start = ((f32[4,1,256,1,8,128]{5,2,0,3,1,4:T(8,128)}), f32[4,1,256,1,8,128]{5,2,0,3,1,4:T(8,128)}, u32[]{:S(2)}, u32[]{:S(2)}) async-start(f32[4,1,256,1,8,128]{5,2,0,3,1,4:T(8,128)} %copy.49), calls=%async_computation | async-start | bytes 8388608 | tf_op jit(solution)/shard_map/all_to_all | solution.py:76
  225.5 48.9 %all-to-all-done = f32[4,1,256,1,8,128]{5,2,0,3,1,4:T(8,128)} async-done(((f32[4,1,256,1,8,128]{5,2,0,3,1,4:T(8,128)}), f32[4,1,256,1,8,128]{5,2,0,3,1,4:T(8,128)}, u32[]{:S(2)}, u32[]{:S(2)}) %all-to-all-start) | async-done | bytes 4194336 | tf_op jit(solution)/shard_map/all_to_all | solution.py:76
  274.5 11.4 %copy.51 = f32[4,8,256,1,1,128]{5,4,3,2,1,0:T(1,128)} copy(f32[4,8,256,1,1,128]{5,2,0,1,4,3:T(8,128)} %bitcast.26) | data formatting | bytes 8388608
  285.8 64.7 %all-gather.6.cloned.1.call-done = f32[512,4,16,256]{3,0,1,2:T(8,128)} async-done(((f32[512,4,1,256]{3,0,1,2:T(8,128)}), f32[512,4,16,256]{3,0,1,2:T(8,128)}) %all-gather.6.cloned.1.call-update) | async-done | bytes 33554448 | tf_op jit(solution)/shard_map/all_gather | solution.py:64
  350.6 28.3 %copy.59 = f32[512,4,16,256]{3,2,1,0:T(8,128)S(1)} copy(f32[512,4,16,256]{3,0,1,2:T(8,128)} %all-gather.6.cloned.1.call-done) | data formatting | bytes 67108864 | tf_op jit(solution)/shard_map/all_gather | solution.py:64
  378.8 6.6 %constant_dynamic-slice_fusion.2 = f32[512,4,2,1,256]{4,3,2,1,0:T(1,128)} fusion(f32[512,4,2,8,256]{4,3,2,1,0:T(8,128)S(1)} %bitcast.106, s32[]{:T(128)S(6)} %select_n.57), kind=kLoop, calls=%fused_computation.59 | loop fusion | bytes 8388612 | tf_op jit(solution)/shard_map/jit(dynamic_index_in_dim)/dynamic_slice | solution.py:68
  385.5 10.9 %copy.41 = f32[512,4,2,1,256]{0,4,2,1,3:T(8,128)} copy(f32[512,4,2,1,256]{4,3,2,1,0:T(1,128)} %constant_dynamic-slice_fusion.2) | data formatting | bytes 8388608 | tf_op jit(solution)/shard_map/jit(dynamic_index_in_dim)/dynamic_slice | solution.py:68
  396.4 17.5 %convolution_multiply_fusion = f32[2048,1024]{1,0:T(8,128)} fusion(f32[512,2048]{0,1:T(8,128)} %bitcast.107, f32[256,1024]{1,0:T(8,128)S(1)} %slice.92, f32[256,1024]{1,0:T(8,128)S(1)} %slice.86), kind=kOutput, calls=%fused_computation.5 | convolution fusion | flops 12887523328 | bytes 14680064 | tf_op jit(solution)/shard_map/dot_general | solution.py:70
  413.9 13.5 %reshape.102 = f32[8,1,256,4,1,256]{5,4,3,2,1,0:T(1,128)} reshape(f32[2048,1024]{1,0:T(8,128)} %convolution_multiply_fusion) | data formatting | bytes 16777216 | tf_op jit(solution)/shard_map/reshape | solution.py:73
  (10 shorter events, 0.1 us)
Async XLA Ops:
  7.2 85.8 %all-gather.8.cloned.1.call-start = ((), (), s32[]{:S(2)}) async-start(), calls=%async_computation.2 | async-start | bytes 9437184 | tf_op jit(solution)/shard_map/all_gather | solution.py:12
  39.2 109.9 %all-gather.10.cloned.1.call-start = ((), (), s32[]{:S(2)}) async-start(), calls=%async_computation.3 | async-start | bytes 9437184 | tf_op jit(solution)/shard_map/all_gather | solution.py:12
  98.8 251.8 %all-gather.6.cloned.1.call-start = ((), (), s32[]{:S(2)}) async-start(), calls=%async_computation.1 | async-start | bytes 35651584 | tf_op jit(solution)/shard_map/all_gather | solution.py:64
  193.6 16.6 %copy-start = (f32[8,256,1024]{1,2,0:T(8,128)S(1)}, f32[8,256,1024]{1,2,0:T(8,128)}, u32[]{:S(2)}) copy-start(f32[8,256,1024]{1,2,0:T(8,128)} %convolution_bitcast_fusion.1) | copy-start | bytes 25165828
  193.6 16.6 %copy-start.1 = (f32[256,1024]{0,1:T(8,128)S(1)}, f32[256,1024]{0,1:T(8,128)}, u32[]{:S(2)}) copy-start(f32[256,1024]{0,1:T(8,128)} %copy.48) | copy-start | bytes 3145732
  220.9 53.6 %all-to-all-start = ((f32[4,1,256,1,8,128]{5,2,0,3,1,4:T(8,128)}), f32[4,1,256,1,8,128]{5,2,0,3,1,4:T(8,128)}, u32[]{:S(2)}, u32[]{:S(2)}) async-start(f32[4,1,256,1,8,128]{5,2,0,3,1,4:T(8,128)} %copy.49), calls=%async_computation | async-start | bytes 8388608 | tf_op jit(solution)/shard_map/all_to_all | solution.py:76
Sparse Core Ops, SparseCore 0:
  39.3 53.6 all-gather.7
  98.9 50.1 all-gather.9
  154.0 196.5 all-gather.5
where the time goes:
time: 441 us; the launch traced here: 434 us
  waiting for transfers between devices  188 us (43%)
  local copies, waits for them, and re-layouts  117 us (27%)
  matrix products  57.8 us (13%)
  other arithmetic  50.2 us (11%)
  between operations  15.5 us (4%)
  starting transfers between devices  5.49 us (1%)
    all_gather x2, waiting for transfers between devices, picked(): lax.all_gather(value, axis)  74.1 us
    all_gather x1, waiting for transfers between devices, per_device(): lax.all_gather(stacked.reshape(depth, blocks_cols, 1, width), 'col', axis...  64.7 us
    all_to_all x1, waiting for transfers between devices, per_device(): lax.all_to_all(finished, 'row', split_axis=4, concat_axis=1, tiled=True)  48.9 us
    another operation x6, other arithmetic, solve_row(): lax.linalg.triangular_solve(diagonal, slab, left_side=True, lower=True)  42.5 us
    dot_general x3, matrix products, eliminate(): jnp.einsum('rab,bc->rac', column_part, solved, precision=lax.Precision.HI...  36.6 us
    unnamed x7, local copies, waits for them, and re-layouts  32.5 us
    all_gather x1, local copies, waits for them, and re-layouts, per_device(): lax.all_gather(stacked.reshape(depth, blocks_cols, 1, width), 'col', axis...  28.3 us
    dynamic_slice x2, local copies, waits for them, and re-layouts, per_device(): chosen = lax.dynamic_index_in_dim(gathered, row_index, 3, keepdims=False)  17.6 us
  transfers between devices with their start and end apart: 4, of which 4 were waited for; matrix products, arithmetic and copies ran while one was open for 24% of the time, Pallas kernels for 0%

commit v1 on v0

--- a/solution.py
+++ b/solution.py
@@ -73,7 +73,16 @@
     gram = (gram * (1.0 / (STEPS * BLK))).reshape(blocks_rows, 1, width, blocks_cols, 1, width)
     finished_count = (K + STEPS) // row_count
     finished = matrix_rows[:finished_count].reshape(finished_count, 1, width, 1, row_count, -1)
-    moved = lax.all_to_all(finished, "row", split_axis=4, concat_axis=1, tiled=True)
+    solve_boxes = lambda buf, group_axis: jnp.concatenate(
+        jax.lax.all_to_all(
+            jnp.stack(jnp.split(buf, jax.lax.axis_size(group_axis), axis=4)),
+            group_axis,
+            split_axis=0,
+            concat_axis=0,
+        ),
+        axis=1,
+    )
+    moved = solve_boxes(finished, "row")
     return (gram, moved)
 
 

time: 441 us -> 442 us (level)
  local copies, waits for them, and re-layouts: 117 us -> 139 us
  waiting for transfers between devices: 188 us -> 168 us
    unnamed x7 -> x30, local copies, waits for them, and re-layouts: 32.5 us -> 57 us
    all_gather x1, waiting for transfers between devices: 64.7 us -> 44.9 us  [per_device(): lax.all_gather(stacked.reshape(depth, blocks_cols, 1, width), 'col', axis...]
    reshape x1 -> x0, local copies, waits for them, and re-layouts: 5.71 us -> none  [per_device(): matrix_rows[:finished_count]]
  transfers between devices with their start and end apart: 4 -> 4, of which waited for: 4 -> 4; matrix products, arithmetic and copies ran while one was open for 24% -> 29% of each run, Pallas kernels for 0% -> 0%
where the time goes in v1:
time: 442 us; the launch traced here: 434 us
  waiting for transfers between devices  168 us (38%)
  local copies, waits for them, and re-layouts  139 us (31%)
  matrix products  57.9 us (13%)
  other arithmetic  48.1 us (11%)
  between operations  15.5 us (4%)
  starting transfers between devices  5.59 us (1%)
    all_gather x2, waiting for transfers between devices, picked(): lax.all_gather(value, axis)  74.1 us
    unnamed x30, local copies, waits for them, and re-layouts  57 us
    all_to_all x1, waiting for transfers between devices, per_device(): jax.lax.all_to_all(jnp.stack(jnp.split(buf, jax.lax.axis_size(group_axis)...  48.9 us
    all_gather x1, waiting for transfers between devices, per_device(): lax.all_gather(stacked.reshape(depth, blocks_cols, 1, width), 'col', axis...  44.9 us
    another operation x6, other arithmetic, solve_row(): lax.linalg.triangular_solve(diagonal, slab, left_side=True, lower=True)  42.5 us
    dot_general x3, matrix products, eliminate(): jnp.einsum('rab,bc->rac', column_part, solved, precision=lax.Precision.HI...  36.7 us
    all_gather x1, local copies, waits for them, and re-layouts, per_device(): lax.all_gather(stacked.reshape(depth, blocks_cols, 1, width), 'col', axis...  28.3 us
    dynamic_slice x2, local copies, waits for them, and re-layouts, per_device(): chosen = lax.dynamic_index_in_dim(gathered, row_index, 3, keepdims=False)  17.6 us
  transfers between devices with their start and end apart: 4, of which 4 were waited for; matrix products, arithmetic and copies ran while one was open for 29% of the time, Pallas kernels for 0%

profile of v1, /device:TPU:1, one launch (start us, length us, event | category | flops | bytes accessed | tf_op | source)
XLA Modules:
  0.0 434.4 jit_solution(11706157244480211859)
XLA Ops:
  7.2 1.1 fusion.16
  8.4 4.0 while.4
  8.4 0.6 fusion.37
  9.0 1.4 bitcast_dynamic-update-slice_fusion.12
  10.4 0.6 fusion.37
  11.0 1.4 bitcast_dynamic-update-slice_fusion.12
  12.4 19.7 %custom-call.4 = f32[2,128,128]{1,2,0:T(8,128)S(1)} custom-call(f32[2,128,128]{2,1,0:T(8,128)S(1)} %get-tuple-element.17), custom_call_target="InvertDiagBlocksLowerTriangular" | custom-call | tf_op jit(solution)/shard_map/triangular_solve/custom-call.1 | solution.py:30
  32.1 4.2 slice_reduce_fusion
  36.4 0.6 fusion.13
  37.1 0.6 convolution_subtract_fusion.1
  37.6 0.6 fusion.22
  38.3 1.0 pad_maximum_fusion.1
  39.4 0.6 all-gather.10.cloned.1.call-start
  39.9 0.6 slice.46
  41.8 0.5 slice.47
  42.4 4.1 while.5
  42.4 0.6 fusion.38
  43.0 1.4 bitcast_dynamic-update-slice_fusion.13
  44.4 0.6 fusion.38
  45.0 1.4 bitcast_dynamic-update-slice_fusion.13
  46.5 19.7 %custom-call.5 = f32[2,128,128]{1,2,0:T(8,128)S(1)} custom-call(f32[2,128,128]{2,1,0:T(8,128)S(1)} %get-tuple-element.18), custom_call_target="InvertDiagBlocksLowerTriangular" | custom-call | tf_op jit(solution)/shard_map/triangular_solve/custom-call.1 | solution.py:30
  66.1 27.0 %all-gather.8.cloned.1.call-done = f32[2048,1024]{1,0:T(8,128)} async-done(((f32[256,1024]{1,0:T(8,128)}), f32[2048,1024]{1,0:T(8,128)}) %all-gather.8.cloned.1.call-update) | async-done | bytes 8388624 | tf_op jit(solution)/shard_map/all_gather | solution.py:12
  93.1 3.0 fusion.8
  96.1 0.6 fusion.11
  96.8 0.6 convolution_subtract_fusion
  97.3 0.6 fusion.20
  98.0 1.0 pad_maximum_fusion.2
  99.3 1.3 slice.86
  100.6 0.5 concatenate.13
  101.1 1.2 copy.59
  102.2 47.1 %all-gather.10.cloned.1.call-done = f32[2048,1024]{1,0:T(8,128)} async-done(((f32[256,1024]{1,0:T(8,128)}), f32[2048,1024]{1,0:T(8,128)}) %all-gather.10.cloned.1.call-update) | async-done | bytes 8388624 | tf_op jit(solution)/shard_map/all_gather | solution.py:12
  149.4 1.3 slice.92
  151.4 2.7 pad_maximum_fusion
  154.2 20.9 %copy.63 = f32[8,1,256,4,1,256]{2,5,3,0,4,1:T(8,128)} copy(f32[8,1,256,4,1,256]{5,4,3,2,1,0:T(1,128)} %param.4) | data formatting | bytes 16777216 | tf_op args[0]
  175.4 17.2 %convolution_bitcast_fusion.1 = f32[8,256,1024]{1,2,0:T(8,128)} fusion(f32[2,8,1,256,256]{4,3,1,2,0:T(8,128)} %bitcast.124, f32[2048,1024]{1,0:T(8,128)} %all-gather.8.cloned.1.call-done), kind=kOutput, calls=%fused_computation.11 | convolution fusion | flops 6442450944 | bytes 11534336 | tf_op jit(solution)/shard_map/rab,bc->rac/dot_general | solution.py:35
  192.6 1.3 copy.69
  193.9 16.5 %convolution_bitcast_fusion = f32[8,256,1024]{1,2,0:T(8,128)S(1)} fusion(f32[2,8,1,256,256]{4,3,1,2,0:T(8,128)} %bitcast.125, f32[2048,1024]{1,0:T(8,128)} %all-gather.10.cloned.1.call-done), kind=kOutput, calls=%fused_computation.10 | convolution fusion | flops 6442450944 | bytes 11534336 | tf_op jit(solution)/shard_map/rab,bc->rac/dot_general | solution.py:35
  210.5 2.8 fusion
  213.3 2.1 fusion.29
  215.4 2.2 copy.85
  217.6 2.1 copy.86
  219.7 2.0 copy.87
  221.7 2.1 copy.88
  223.8 2.0 copy.89
  225.8 2.0 copy.90
  227.9 1.0 copy.91
  228.9 1.0 copy.92
  229.9 2.0 bitcast_dynamic-update-slice_fusion.9
  231.9 1.9 bitcast_dynamic-update-slice_fusion.8
  233.8 1.9 bitcast_dynamic-update-slice_fusion.7
  235.6 1.9 bitcast_dynamic-update-slice_fusion.6
  237.5 0.8 bitcast_dynamic-update-slice_fusion.5
  238.3 0.8 bitcast_dynamic-update-slice_fusion.4
  239.2 0.8 bitcast_dynamic-update-slice_fusion.3
  240.0 0.8 bitcast_dynamic-update-slice_fusion.2
  240.8 4.8 %all-to-all-start = ((f32[8,4,1,256,1,1,128]{6,3,1,5,4,2,0:T(8,128)}), f32[8,4,1,256,1,1,128]{6,3,1,5,4,2,0:T(8,128)}, u32[]{:S(2)}, u32[]{:S(2)}) async-start(f32[8,4,1,256,1,1,128]{6,3,1,5,4,2,0:T(8,128)} %bitcast_dynamic-update-slice_fusion.2), calls=%async_computation | async-start | bytes 8388608 | tf_op jit(solution)/shard_map/all_to_all | solution.py:77
  245.6 48.9 %all-to-all-done = f32[8,4,1,256,1,1,128]{6,3,1,5,4,2,0:T(8,128)} async-done(((f32[8,4,1,256,1,1,128]{6,3,1,5,4,2,0:T(8,128)}), f32[8,4,1,256,1,1,128]{6,3,1,5,4,2,0:T(8,128)}, u32[]{:S(2)}, u32[]{:S(2)}) %all-to-all-start) | async-done | bytes 4194336 | tf_op jit(solution)/shard_map/all_to_all | solution.py:77
  294.5 11.4 %copy.79 = f32[4,8,256,1,1,128]{5,4,3,2,1,0:T(1,128)} copy(f32[4,8,256,1,1,128]{5,2,0,1,4,3:T(8,128)} %bitcast.33) | data formatting | bytes 8388608
  305.9 44.9 %all-gather.6.cloned.1.call-done = f32[512,4,16,256]{3,0,1,2:T(8,128)} async-done(((f32[512,4,1,256]{3,0,1,2:T(8,128)}), f32[512,4,16,256]{3,0,1,2:T(8,128)}) %all-gather.6.cloned.1.call-update) | async-done | bytes 33554448 | tf_op jit(solution)/shard_map/all_gather | solution.py:64
  350.8 28.3 %copy.95 = f32[512,4,16,256]{3,2,1,0:T(8,128)S(1)} copy(f32[512,4,16,256]{3,0,1,2:T(8,128)} %all-gather.6.cloned.1.call-done) | data formatting | bytes 67108864 | tf_op jit(solution)/shard_map/all_gather | solution.py:64
  379.1 6.6 %constant_dynamic-slice_fusion.2 = f32[512,4,2,1,256]{4,3,2,1,0:T(1,128)} fusion(f32[512,4,2,8,256]{4,3,2,1,0:T(8,128)S(1)} %bitcast.120, s32[]{:T(128)S(6)} %select_n.57), kind=kLoop, calls=%fused_computation.67 | loop fusion | bytes 8388612 | tf_op jit(solution)/shard_map/jit(dynamic_index_in_dim)/dynamic_slice | solution.py:68
  385.7 10.9 %copy.62 = f32[512,4,2,1,256]{0,4,2,1,3:T(8,128)} copy(f32[512,4,2,1,256]{4,3,2,1,0:T(1,128)} %constant_dynamic-slice_fusion.2) | data formatting | bytes 8388608 | tf_op jit(solution)/shard_map/jit(dynamic_index_in_dim)/dynamic_slice | solution.py:68
  396.7 17.5 %convolution_multiply_fusion = f32[2048,1024]{1,0:T(8,128)} fusion(f32[512,2048]{0,1:T(8,128)} %bitcast.121, f32[256,1024]{1,0:T(8,128)S(1)} %slice.92, f32[256,1024]{1,0:T(8,128)S(1)} %slice.86), kind=kOutput, calls=%fused_computation.5 | convolution fusion | flops 12887523328 | bytes 14680064 | tf_op jit(solution)/shard_map/dot_general | solution.py:70
  414.2 13.5 %reshape.110 = f32[8,1,256,4,1,256]{5,4,3,2,1,0:T(1,128)} reshape(f32[2048,1024]{1,0:T(8,128)} %convolution_multiply_fusion) | data formatting | bytes 16777216 | tf_op jit(solution)/shard_map/reshape | solution.py:73
  (32 shorter events, 1.7 us)
Async XLA Ops:
  7.2 86.0 %all-gather.8.cloned.1.call-start = ((), (), s32[]{:S(2)}) async-start(), calls=%async_computation.2 | async-start | bytes 9437184 | tf_op jit(solution)/shard_map/all_gather | solution.py:12
  39.4 110.0 %all-gather.10.cloned.1.call-start = ((), (), s32[]{:S(2)}) async-start(), calls=%async_computation.3 | async-start | bytes 9437184 | tf_op jit(solution)/shard_map/all_gather | solution.py:12
  99.0 251.8 %all-gather.6.cloned.1.call-start = ((), (), s32[]{:S(2)}) async-start(), calls=%async_computation.1 | async-start | bytes 35651584 | tf_op jit(solution)/shard_map/all_gather | solution.py:64
  193.9 16.6 %copy-start = (f32[8,256,1024]{1,2,0:T(8,128)S(1)}, f32[8,256,1024]{1,2,0:T(8,128)}, u32[]{:S(2)}) copy-start(f32[8,256,1024]{1,2,0:T(8,128)} %convolution_bitcast_fusion.1) | copy-start | bytes 25165828
  193.9 16.6 %copy-start.1 = (f32[256,1024]{0,1:T(8,128)S(1)}, f32[256,1024]{0,1:T(8,128)}, u32[]{:S(2)}) copy-start(f32[256,1024]{0,1:T(8,128)} %copy.69) | copy-start | bytes 3145732
  228.9 10.3 %copy-start.2 = (f32[4,1,256,1,1,128]{5,2,0,4,3,1:T(8,128)S(1)}, f32[4,1,256,1,1,128]{5,2,0,4,3,1:T(8,128)}, u32[]{:S(2)}) copy-start(f32[4,1,256,1,1,128]{5,2,0,4,3,1:T(8,128)} %copy.91) | copy-start | bytes 1572868
  229.9 7.6 %copy-start.5 = (f32[4,1,256,1,1,128]{5,2,0,4,3,1:T(8,128)S(1)}, f32[4,1,256,1,1,128]{5,2,0,4,3,1:T(8,128)}, u32[]{:S(2)}) copy-start(f32[4,1,256,1,1,128]{5,2,0,4,3,1:T(8,128)} %copy.89) | copy-start | bytes 1572868
  229.9 8.5 %copy-start.4 = (f32[4,1,256,1,1,128]{5,2,0,4,3,1:T(8,128)S(1)}, f32[4,1,256,1,1,128]{5,2,0,4,3,1:T(8,128)}, u32[]{:S(2)}) copy-start(f32[4,1,256,1,1,128]{5,2,0,4,3,1:T(8,128)} %copy.90) | copy-start | bytes 1572868
  229.9 10.1 %copy-start.3 = (f32[4,1,256,1,1,128]{5,2,0,4,3,1:T(8,128)S(1)}, f32[4,1,256,1,1,128]{5,2,0,4,3,1:T(8,128)}, u32[]{:S(2)}) copy-start(f32[4,1,256,1,1,128]{5,2,0,4,3,1:T(8,128)} %copy.92) | copy-start | bytes 1572868
  240.8 53.7 %all-to-all-start = ((f32[8,4,1,256,1,1,128]{6,3,1,5,4,2,0:T(8,128)}), f32[8,4,1,256,1,1,128]{6,3,1,5,4,2,0:T(8,128)}, u32[]{:S(2)}, u32[]{:S(2)}) async-start(f32[8,4,1,256,1,1,128]{6,3,1,5,4,2,0:T(8,128)} %bitcast_dynamic-update-slice_fusion.2), calls=%async_computation | async-start | bytes 8388608 | tf_op jit(solution)/shard_map/all_to_all | solution.py:77
Sparse Core Ops, SparseCore 0:
  39.5 53.6 all-gather.7
  99.2 50.1 all-gather.9
  154.3 196.5 all-gather.5
